TPU v7x, 32 devices: a whole 2x2x4 slice. The times are simulated.
32 devices in a mesh: groups: 2 (over y), row: 4 (over z), col: 4 (over x, core).
Axes of the slice: x: 2, y: 2, z: 4, core: 2. Of those that a mesh axis runs over, the one named last changes fastest.
Arguments:
- node_embed: bfloat16 [384, 256], P(('groups', 'row')), parts along dimension 0, may hold values from -6 to 6
- rotation: float32 [3, 3, 384], P(None, None, 'groups'), parts along dimension 2, may hold values from -1 to 1, as said below
- translation: float32 [3, 384], P(None, 'groups'), parts along dimension 1, may hold values from -8 to 8
- pair_embed: bfloat16 [384, 192, 128], P(('groups', 'row'), 'col'), parts along dimension 0, may hold values from -1300 to 1300
- chain_index: int32 [384], P('groups'), parts along dimension 0, may hold values from 0 to 7, never falling along the last dimension, each value on 1 to 48 neighbouring positions
- residue_mask: int32 [384], P('groups'), parts along dimension 0, may hold values 0 or 1
- step_index: int32 [2], P('groups'), parts along dimension 0, may hold values from 0 to 999
- w_time: bfloat16 [256, 256], replicated, may hold values from -0.375 to 0.375
- w_query: bfloat16 [256, 2048], replicated, may hold values from -0.375 to 0.375
- w_query_points: bfloat16 [256, 192], replicated, may hold values from -0.375 to 0.375
- w_kv: bfloat16 [256, 4096], replicated, may hold values from -0.375 to 0.375
- w_kvp: bfloat16 [256, 480], replicated, may hold values from -0.375 to 0.375
- w_bias: bfloat16 [128, 8], replicated, may hold values from -0.5 to 0.5
- head_weights: float32 [8], replicated, may hold values from -1 to 1.5
- chain_bias: float32 [8], replicated, may hold values from -2 to 2
- w_out: bfloat16 [3456, 256], replicated, may hold values from -0.109375 to 0.109375
- w_mlp_in: bfloat16 [256, 256], replicated, may hold values from -0.375 to 0.375
- w_mlp_out: bfloat16 [256, 256], replicated, may hold values from -0.375 to 0.375
- w_edge_in: bfloat16 [256, 128], replicated, may hold values from -0.375 to 0.375
- w_trunk_in: bfloat16 [384, 384], replicated, may hold values from -0.3125 to 0.3125
- w_trunk_mid: bfloat16 [384, 384], replicated, may hold values from -0.3125 to 0.3125
- w_final: bfloat16 [384, 128], replicated, may hold values from -0.3125 to 0.3125
Outputs:
- node_out: bfloat16 [384, 256], P(('groups', 'row')), parts along dimension 0
- pair_out: bfloat16 [384, 192, 128], P(('groups', 'row'), 'col'), parts along dimension 0
There are 2 independent parts, one for each index of `groups`. A program takes and returns all parts, laid end to end along the dimension named above; an argument that names none is the same for every part. Nothing has to cross between parts.
Inputs may be any that keep to these rules, and one draw needn't show every extreme that they name: Each rotation[:, :, n] is a proper rotation matrix. `chain_index`: chain ids never fall along the residues; each chain has 1 to 48 residues, one exactly that many.
All inputs are finite; a program needn't handle non-finite values.
Results may differ from a plain program's by a relative error of at most 0.012.
Values may be sent and summed in bfloat16 or wider, within the bound.
No kernel may reach another device: no remote copies, remote signals or barrier semaphores. Data moves between devices by JAX's collectives and lax.ppermute only.
A program may use at most 64 MiB of HBM per device.

v0:
```python
import math
import jax
import jax.numpy as jnp
from jax import lax
from jax.sharding import PartitionSpec as P

CS = 256
CZ = 128
HEADS = 8
CH = 256
QP = 8
VP = 12
NH = 128
HID = 384
norm_epsilon = 1e-05
masked_score = 100000.0
highest = lax.Precision.HIGHEST


def layer_norm(values):
    average = jnp.mean(values, -1, keepdims=True)
    centred = values - average
    spread = jnp.mean(centred * centred, -1, keepdims=True)
    return centred * lax.rsqrt(spread + norm_epsilon)


def time_embedding(step_index, embed_width):
    half_width = embed_width // 2
    frequency = jnp.exp(-math.log(10000.0) * jnp.arange(half_width, dtype=jnp.float32) / half_width)
    angles = step_index.astype(jnp.float32)[0] * frequency
    return jnp.concatenate([jnp.sin(angles), jnp.cos(angles)])[None, :].astype(jnp.bfloat16)


def to_global(rotation, shift_vec, points):
    turned = jnp.einsum("abn,nbm->nam", rotation, points, precision=highest)
    return turned + jnp.transpose(shift_vec)[:, :, None]


def project_keys(embedded, rotation, shift_vec, w_kv, w_kvp):
    item_count = embedded.shape[0]
    key_values = jnp.dot(embedded, w_kv, preferred_element_type=jnp.float32).astype(jnp.bfloat16)
    points = jnp.dot(embedded, w_kvp, preferred_element_type=jnp.float32).reshape(item_count, 3, -1)
    return (key_values, to_global(rotation, shift_vec, points))


def node_finish(
    denominator,
    values_out,
    points_out,
    pair_sums,
    embedded,
    rotation,
    shift_vec,
    mask_rows,
    w_out,
    w_mlp_in,
    w_mlp_out,
    w_edge_in,
):
    item_count = embedded.shape[0]
    scale_back = denominator[:, :, None]
    attended = values_out.reshape(item_count, HEADS, CH) / scale_back
    points = points_out.reshape(item_count, 3, HEADS, VP) / denominator[:, None, :, None]
    relative = points - jnp.transpose(shift_vec)[:, :, None, None]
    framed = jnp.einsum("abi,iahv->ibhv", rotation, relative, precision=highest)
    length = jnp.sqrt(jnp.maximum(jnp.sum(framed * framed, 1), 1.0))
    paired = pair_sums.reshape(item_count, HEADS, CZ) / scale_back
    features = jnp.concatenate(
        [
            attended.reshape(item_count, -1),
            framed.reshape(item_count, -1),
            length.reshape(item_count, -1),
            paired.reshape(item_count, -1),
        ],
        -1,
    ).astype(jnp.bfloat16)
    update = jnp.dot(features, w_out, preferred_element_type=jnp.float32)
    normed = layer_norm(embedded.astype(jnp.float32) + update).astype(jnp.bfloat16)
    normed = lax.optimization_barrier(normed)
    middle = jax.nn.relu(jnp.dot(normed, w_mlp_in, preferred_element_type=jnp.float32)).astype(
        jnp.bfloat16
    )
    node_new = layer_norm(
        normed.astype(jnp.float32) + jnp.dot(middle, w_mlp_out, preferred_element_type=jnp.float32)
    )
    node_new = (node_new * mask_rows.astype(jnp.float32)[:, None]).astype(jnp.bfloat16)
    edge_side = jnp.dot(node_new, w_edge_in, preferred_element_type=jnp.float32).astype(
        jnp.bfloat16
    )
    return (node_new, edge_side)


def body(
    node_embed,
    rotation,
    translation,
    pair_embed,
    chain_index,
    residue_mask,
    step_index,
    w_time,
    w_query,
    w_query_points,
    w_kv,
    w_kvp,
    w_bias,
    head_weights,
    chain_bias,
    w_out,
    w_mlp_in,
    w_mlp_out,
    w_edge_in,
    w_trunk_in,
    w_trunk_mid,
    w_final,
):
    row_count = node_embed.shape[0]
    key_count = pair_embed.shape[1]
    row_start = lax.axis_index("row") * row_count
    key_start = lax.axis_index("col") * key_count
    embedded = (
        node_embed.astype(jnp.float32)
        + jnp.dot(time_embedding(step_index, CS), w_time, preferred_element_type=jnp.float32)
    ).astype(jnp.bfloat16)
    embedded = lax.optimization_barrier(embedded)
    rot_rows = lax.dynamic_slice_in_dim(rotation, row_start, row_count, 2)
    shift_rows = lax.dynamic_slice_in_dim(translation, row_start, row_count, 1)
    mask_rows = lax.dynamic_slice_in_dim(residue_mask, row_start, row_count, 0)
    mask_keys = lax.dynamic_slice_in_dim(residue_mask, key_start, key_count, 0)
    chain_rows = lax.dynamic_slice_in_dim(chain_index, row_start, row_count, 0)
    chain_keys = lax.dynamic_slice_in_dim(chain_index, key_start, key_count, 0)
    query_feat = (
        jnp.dot(embedded, w_query, preferred_element_type=jnp.float32)
        .astype(jnp.bfloat16)
        .reshape(row_count, HEADS, CH)
    )
    query_pts = to_global(
        rot_rows,
        shift_rows,
        jnp.dot(embedded, w_query_points, preferred_element_type=jnp.float32).reshape(
            row_count, 3, HEADS * QP
        ),
    ).reshape(row_count, 3, HEADS, QP)
    all_nodes = lax.all_gather(embedded, "row", axis=0, tiled=True)
    key_nodes = lax.dynamic_slice_in_dim(all_nodes, key_start, key_count, 0)
    rot_keys = lax.dynamic_slice_in_dim(rotation, key_start, key_count, 2)
    shift_keys = lax.dynamic_slice_in_dim(translation, key_start, key_count, 1)
    key_values, key_points = project_keys(key_nodes, rot_keys, shift_keys, w_kv, w_kvp)
    key_feat = key_values[:, : HEADS * CH].reshape(key_count, HEADS, CH)
    value_feat = key_values[:, HEADS * CH :].reshape(key_count, HEADS, CH)
    key_points = key_points.reshape(key_count, 3, HEADS, QP + VP)
    key_pts = key_points[..., :QP]
    value_pts = key_points[..., QP:]
    scaled = math.sqrt(1.0 / 3.0)
    point_weight = math.sqrt(2.0 / (9.0 * QP))
    point_gain = jax.nn.softplus(head_weights)
    feature_dots = jnp.einsum(
        "ihc,jhc->hij", query_feat, key_feat, preferred_element_type=jnp.float32
    ) / math.sqrt(CH)
    pair_bias = jnp.einsum("ijc,ch->hij", pair_embed, w_bias, preferred_element_type=jnp.float32)
    same_chain = (chain_rows[:, None] == chain_keys[None, :]).astype(jnp.float32)
    query_square = jnp.einsum("iahp,iahp->hi", query_pts, query_pts, precision=highest)
    key_square = jnp.einsum("jahp,jahp->hj", key_pts, key_pts, precision=highest)
    cross_term = jnp.einsum("iahp,jahp->hij", query_pts, key_pts, precision=highest)
    distance = query_square[:, :, None] + key_square[:, None, :] - 2.0 * cross_term
    mask_term = (mask_keys.astype(jnp.float32) - 1.0) * masked_score
    scores = (
        scaled * (feature_dots + pair_bias + chain_bias[:, None, None] * same_chain[None])
        - scaled * point_weight * 0.5 * point_gain[:, None, None] * distance
        + mask_term[None, None, :]
    )
    row_peak = lax.pmax(jnp.max(scores, -1), "col")
    weights = jnp.exp(scores - row_peak[:, :, None])
    denominator = jnp.transpose(jnp.sum(weights, -1))
    rounded = weights.astype(jnp.bfloat16)
    values_out = jnp.einsum(
        "hij,jhc->ihc", rounded, value_feat, preferred_element_type=jnp.float32
    ).reshape(row_count, -1)
    points_out = jnp.einsum("hij,jahv->iahv", weights, value_pts, precision=highest).reshape(
        row_count, -1
    )
    pair_sums = jnp.einsum(
        "hij,ijc->ihc", rounded, pair_embed, preferred_element_type=jnp.float32
    ).reshape(row_count, -1)
    summed = lax.psum((denominator, values_out, points_out, pair_sums), "col")
    node_out, edge_side = node_finish(
        summed[0],
        summed[1],
        summed[2],
        summed[3],
        embedded,
        rot_rows,
        shift_rows,
        mask_rows,
        w_out,
        w_mlp_in,
        w_mlp_out,
        w_edge_in,
    )
    side_all = lax.all_gather(edge_side, "row", axis=0, tiled=True)
    side_rows = lax.dynamic_slice_in_dim(side_all, row_start, row_count, 0)
    side_keys = lax.dynamic_slice_in_dim(side_all, key_start, key_count, 0)
    pre_rows = jnp.dot(side_rows, w_trunk_in[CZ : CZ + NH], preferred_element_type=jnp.float32)
    pre_keys = jnp.dot(side_keys, w_trunk_in[CZ + NH :], preferred_element_type=jnp.float32)
    mask_key_f = mask_keys.astype(jnp.float32)
    block_rows = math.gcd(row_count, 8)
    block_count = row_count // block_rows

    def edge_block(inputs):
        pair_block, pre_block, side_block, keep_block = inputs
        lifted = (
            jnp.einsum(
                "ijc,cd->ijd", pair_block, w_trunk_in[:CZ], preferred_element_type=jnp.float32
            )
            + pre_block[:, None, :]
            + pre_keys[None, :, :]
        )
        hidden_one = jax.nn.relu(lifted).astype(jnp.bfloat16)
        hidden_two = jax.nn.relu(
            jnp.einsum("ijd,de->ije", hidden_one, w_trunk_mid, preferred_element_type=jnp.float32)
        )
        stacked = jnp.concatenate(
            [
                pair_block,
                jnp.broadcast_to(side_block[:, None, :], (block_rows, key_count, NH)),
                jnp.broadcast_to(side_keys[None, :, :], (block_rows, key_count, NH)),
            ],
            -1,
        )
        joined = (hidden_two + stacked.astype(jnp.float32)).astype(jnp.bfloat16)
        edge_out = jnp.einsum("ijd,dc->ijc", joined, w_final, preferred_element_type=jnp.float32)
        pair_keep = keep_block.astype(jnp.float32)[:, None] * mask_key_f[None, :]
        return (layer_norm(edge_out) * pair_keep[:, :, None]).astype(jnp.bfloat16)

    pair_out = lax.map(
        edge_block,
        (
            pair_embed.reshape(block_count, block_rows, key_count, CZ),
            pre_rows.reshape(block_count, block_rows, HID),
            side_rows.reshape(block_count, block_rows, NH),
            mask_rows.reshape(block_count, block_rows),
        ),
    )
    return (node_out, pair_out.reshape(row_count, key_count, CZ))


def solution(mesh):
    return jax.shard_map(
        body,
        mesh=mesh,
        in_specs=(
            P(("groups", "row"), None),
            P(None, None, "groups"),
            P(None, "groups"),
            P(("groups", "row"), "col", None),
            P("groups"),
            P("groups"),
            P("groups"),
            P(),
            P(),
            P(),
            P(),
            P(),
            P(),
            P(),
            P(),
            P(),
            P(),
            P(),
            P(),
            P(),
            P(),
            P(),
        ),
        out_specs=(P(("groups", "row"), None), P(("groups", "row"), "col", None)),
        check_vma=False,
    )
```

profile of v0, /device:TPU:0, one launch (start us, length us, event | category | flops | bytes accessed | tf_op | source)
XLA Modules:
  0.0 135.2 jit_solution(5228488410972986476)
XLA Ops:
  8.0 1.2 fusion.59
  9.3 1.3 add_multiply_fusion
  10.6 1.4 %fusion.61 = (f32[48]{0:T(128)}, s32[48]{0:T(128)}, s32[48]{0:T(128)}, s32[48]{0:T(128)}) fusion(s32[192]{0:T(256)} %param.29, s32[]{:T(128)S(6)} %select_n.8, s32[192]{0:T(256)} %param.28, s32[]{:T(128)S(6)} %select_n.7), kind=kLoop, calls=%fused_computation.115 | loop fusion | flops 48 | bytes 1352 | tf_op jit(solution)/shard_map/convert_element_type | solution.py:86
  12.1 0.8 dynamic-slice_bitcast_fusion.4
  12.9 0.9 constant_dynamic-slice_fusion.2
  13.8 1.0 fusion.68
  14.9 0.8 add_convert_fusion
  15.7 15.0 %all_gather.6 = bf16[192,256]{1,0:T(8,128)(2,1)S(1)} all-gather(bf16[48,256]{1,0:T(8,128)(2,1)S(1)} %add_convert_fusion), channel_id=1, replica_groups=mesh['groups'=2,'row'=4,'col'=4] {'row'}, dimensions={0}, use_global_device_ids=true | all-gather | bytes 122880 | tf_op jit(solution)/shard_map/all_gather | solution.py:144
  30.7 1.1 fusion.69
  32.2 0.4 convolution_add_fusion.2
  32.8 0.6 fusion.42
  33.4 1.1 fusion.50
  34.7 0.5 convolution_add_fusion.1
  35.4 1.5 %convolution_convert_fusion.1 = bf16[48,2048]{1,0:T(8,128)(2,1)S(1)} fusion(bf16[48,256]{1,0:T(8,128)(2,1)S(1)} %add_convert_fusion, bf16[256,2048]{1,0:T(8,128)(2,1)} %param.32), kind=kOutput, calls=%fused_computation.30 | convolution fusion | flops 50429952 | bytes 1269760 | tf_op jit(solution)/shard_map/dot_general | solution.py:133
  37.0 1.3 fusion.54
  38.3 0.8 copy.83
  39.1 1.3 convolution_convert_fusion
  40.4 0.7 fusion.63
  41.2 1.1 fusion.27
  42.6 5.7 %pmax.7 = f32[8,48]{1,0:T(8,128)S(1)} all-reduce(f32[8,48]{1,0:T(8,128)S(1)} %get-tuple-element.115), channel_id=1, replica_groups=mesh['groups'=2,'row'=4,'col'=4] {'col'}, use_global_device_ids=true, to_apply=%region_1.2 | all-reduce | flops 384 | bytes 3072 | tf_op jit(solution)/shard_map/pmax | solution.py:172
  48.5 1.2 convolution_bitcast_fusion
  49.6 0.8 copy.131
  50.4 0.3 fusion.70
  50.7 0.7 copy.155
  51.4 0.3 convolution_bitcast_fusion.1
  51.8 15.2 %all-reduce = (f32[48,8]{0,1:T(8,128)S(1)}, f32[48,3,8,12]{0,3,1,2:T(8,128)S(1)}) all-reduce(f32[48,8]{0,1:T(8,128)S(1)} %bitcast.172, f32[48,3,8,12]{0,3,1,2:T(8,128)S(1)} %convolution_bitcast_fusion.1), channel_id=1, replica_groups=mesh['groups'=2,'row'=4,'col'=4] {'col'}, use_global_device_ids=true, to_apply=%region_4.5 | all-reduce | flops 14208 | bytes 113664 | tf_op jit(solution)/shard_map/psum | solution.py:185
  67.0 0.7 divide_subtract_fusion
  67.7 1.8 %copy.97 = f32[48,3,8,12]{3,1,2,0:T(4,128)S(1)} copy(f32[48,3,8,12]{0,3,1,2:T(8,128)} %divide_subtract_fusion) | data formatting | bytes 110592 | tf_op jit(solution)/shard_map/sub | solution.py:64
  69.5 4.5 %multiply_reduce_fusion.1 = (f32[48,8,12]{2,1,0:T(8,128)}, bf16[48,3,8,12]{3,1,2,0:T(4,128)(2,1)}) fusion(f32[48,3,8,12]{3,1,2,0:T(4,128)S(1)} %copy.97, f32[3,3,48]{1,0,2:T(4,128)} %copy-done.4), kind=kOutput, calls=%fused_computation.51 | convolution fusion | flops 534528 | bytes 103104 | tf_op jit(solution)/shard_map/abi,iahv->ibhv/dot_general | solution.py:65
  74.4 1.1 copy.99
  75.6 1.5 %copy.98 = bf16[48,3,8,12]{0,3,2,1:T(8,128)(2,1)S(1)} copy(bf16[48,3,8,12]{3,1,2,0:T(4,128)(2,1)} %get-tuple-element.102) | data formatting | bytes 55296 | tf_op jit(solution)/shard_map/convert.5
  77.2 10.0 %all-reduce.4.cloned.1.call-done = (f32[48,2048]{1,0:T(8,128)}, f32[48,1024]{1,0:T(8,128)}) async-done(((f32[48,2048]{1,0:T(8,128)}, f32[48,1024]{1,0:T(8,128)}), (f32[48,2048]{1,0:T(8,128)}, f32[48,1024]{1,0:T(8,128)})) %all-reduce.4.cloned.1.call-update) | async-done | bytes 589840 | tf_op jit(solution)/shard_map/psum | solution.py:185
  87.3 1.0 fusion.29
  88.3 1.1 divide_convert_fusion
  89.5 2.0 %fusion.66 = (f32[48]{0:T(128)S(1)}, f32[48,256]{1,0:T(8,128)S(1)}) fusion(bf16[48,3456]{1,0:T(8,128)(2,1)S(1)} %concatenate.14, bf16[3456,256]{1,0:T(8,128)(2,1)} %param.39, bf16[48,256]{1,0:T(8,128)(2,1)S(1)} %add_convert_fusion), kind=kOutput, calls=%fused_computation.120 | convolution fusion | flops 84971472 | bytes 2175168 | tf_op jit(solution)/shard_map/dot_general | solution.py:77
  91.8 0.4 fusion.67
  92.5 1.0 convolution_convert_fusion.2
  93.5 13.2 %all_gather.7 = bf16[192,128]{1,0:T(8,128)(2,1)S(1)} all-gather(bf16[48,128]{1,0:T(8,128)(2,1)S(1)} %convolution_convert_fusion.2), channel_id=1, replica_groups=mesh['groups'=2,'row'=4,'col'=4] {'row'}, dimensions={0}, use_global_device_ids=true | all-gather | bytes 61440 | tf_op jit(solution)/shard_map/all_gather | solution.py:200
  106.7 1.0 convolution_bitcast_fusion.3
  107.7 1.7 %fusion.44 = f32[48,384]{1,0:T(8,128)} fusion(bf16[48,128]{1,0:T(8,128)(2,1)S(1)} %get-tuple-element.215, bf16[384,384]{1,0:T(8,128)(2,1)} %param.43), kind=kOutput, calls=%fused_computation.74 | convolution fusion | flops 4718592 | bytes 184320 | tf_op jit(solution)/shard_map/dot_general | solution.py:204
  109.4 18.9 %while.10 = (s32[]{:T(128)}, bf16[6,8,48,128]{3,2,1,0:T(8,128)(2,1)}, bf16[6,8,48,128]{3,2,1,0:T(8,128)(2,1)S(1)}, bf16[384,384]{1,0:T(8,128)(2,1)}, f32[6,8,384...) while((s32[]{:T(128)}, ...), condition=%wide.region_15.16_spmd, body=%wide.region_12.15_spmd.sunk | while | flops 191054592 | bytes 2702265 | solution.py:235
  109.5 1.5 %fusion.111 = bf16[8,48,384]{2,1,0:T(8,128)(2,1)S(1)} fusion(bf16[8,48,128]{2,1,0:T(8,128)(2,1)S(1)} %dynamic-slice_bitcast_fusion.9, bf16[8,48,128]{2,1,0:T(8,128)(2,1)S(1)} %broadcast_in_dim.14, bf16[8,48,128]{2,1,0:T(8,128)(2,1)S(1)} %broadcast_in_dim.15, bf16[384,384]{1,0:T(8,128)(2,1)} %get-tuple-element.239, f32[48,384]{1,0:T(8,128)} %get-tuple-element.238, ...), kind=kOutput, calls=%fused_computation.6.clone.1 | convolution fusion | flops 152911872 | bytes 1167360 | tf_op jit(solution)/shard_map/while/body/eval_jaxpr/ijd,de->ije/dot_general | solution.py:220
  111.1 0.3 fusion.112
  111.4 0.2 multiply_reduce_fusion.6
  111.7 0.9 fusion.114
  112.7 1.5 %fusion.111 = bf16[8,48,384]{2,1,0:T(8,128)(2,1)S(1)} fusion(bf16[8,48,128]{2,1,0:T(8,128)(2,1)S(1)} %dynamic-slice_bitcast_fusion.9, bf16[8,48,128]{2,1,0:T(8,128)(2,1)S(1)} %broadcast_in_dim.14, bf16[8,48,128]{2,1,0:T(8,128)(2,1)S(1)} %broadcast_in_dim.15, bf16[384,384]{1,0:T(8,128)(2,1)} %get-tuple-element.239, f32[48,384]{1,0:T(8,128)} %get-tuple-element.238, ...), kind=kOutput, calls=%fused_computation.6.clone.1 | convolution fusion | flops 152911872 | bytes 1167360 | tf_op jit(solution)/shard_map/while/body/eval_jaxpr/ijd,de->ije/dot_general | solution.py:220
  114.2 0.3 fusion.112
  114.6 0.2 multiply_reduce_fusion.6
  114.9 0.9 fusion.114
  115.8 1.5 %fusion.111 = bf16[8,48,384]{2,1,0:T(8,128)(2,1)S(1)} fusion(bf16[8,48,128]{2,1,0:T(8,128)(2,1)S(1)} %dynamic-slice_bitcast_fusion.9, bf16[8,48,128]{2,1,0:T(8,128)(2,1)S(1)} %broadcast_in_dim.14, bf16[8,48,128]{2,1,0:T(8,128)(2,1)S(1)} %broadcast_in_dim.15, bf16[384,384]{1,0:T(8,128)(2,1)} %get-tuple-element.239, f32[48,384]{1,0:T(8,128)} %get-tuple-element.238, ...), kind=kOutput, calls=%fused_computation.6.clone.1 | convolution fusion | flops 152911872 | bytes 1167360 | tf_op jit(solution)/shard_map/while/body/eval_jaxpr/ijd,de->ije/dot_general | solution.py:220
  117.4 0.3 fusion.112
  117.7 0.2 multiply_reduce_fusion.6
  118.0 0.9 fusion.114
  119.0 1.5 %fusion.111 = bf16[8,48,384]{2,1,0:T(8,128)(2,1)S(1)} fusion(bf16[8,48,128]{2,1,0:T(8,128)(2,1)S(1)} %dynamic-slice_bitcast_fusion.9, bf16[8,48,128]{2,1,0:T(8,128)(2,1)S(1)} %broadcast_in_dim.14, bf16[8,48,128]{2,1,0:T(8,128)(2,1)S(1)} %broadcast_in_dim.15, bf16[384,384]{1,0:T(8,128)(2,1)} %get-tuple-element.239, f32[48,384]{1,0:T(8,128)} %get-tuple-element.238, ...), kind=kOutput, calls=%fused_computation.6.clone.1 | convolution fusion | flops 152911872 | bytes 1167360 | tf_op jit(solution)/shard_map/while/body/eval_jaxpr/ijd,de->ije/dot_general | solution.py:220
  120.5 0.3 fusion.112
  120.9 0.2 multiply_reduce_fusion.6
  121.2 0.9 fusion.114
  122.1 1.5 %fusion.111 = bf16[8,48,384]{2,1,0:T(8,128)(2,1)S(1)} fusion(bf16[8,48,128]{2,1,0:T(8,128)(2,1)S(1)} %dynamic-slice_bitcast_fusion.9, bf16[8,48,128]{2,1,0:T(8,128)(2,1)S(1)} %broadcast_in_dim.14, bf16[8,48,128]{2,1,0:T(8,128)(2,1)S(1)} %broadcast_in_dim.15, bf16[384,384]{1,0:T(8,128)(2,1)} %get-tuple-element.239, f32[48,384]{1,0:T(8,128)} %get-tuple-element.238, ...), kind=kOutput, calls=%fused_computation.6.clone.1 | convolution fusion | flops 152911872 | bytes 1167360 | tf_op jit(solution)/shard_map/while/body/eval_jaxpr/ijd,de->ije/dot_general | solution.py:220
  123.7 0.3 fusion.112
  124.0 0.2 multiply_reduce_fusion.6
  124.3 0.9 fusion.114
  125.3 1.5 %fusion.111 = bf16[8,48,384]{2,1,0:T(8,128)(2,1)S(1)} fusion(bf16[8,48,128]{2,1,0:T(8,128)(2,1)S(1)} %dynamic-slice_bitcast_fusion.9, bf16[8,48,128]{2,1,0:T(8,128)(2,1)S(1)} %broadcast_in_dim.14, bf16[8,48,128]{2,1,0:T(8,128)(2,1)S(1)} %broadcast_in_dim.15, bf16[384,384]{1,0:T(8,128)(2,1)} %get-tuple-element.239, f32[48,384]{1,0:T(8,128)} %get-tuple-element.238, ...), kind=kOutput, calls=%fused_computation.6.clone.1 | convolution fusion | flops 152911872 | bytes 1167360 | tf_op jit(solution)/shard_map/while/body/eval_jaxpr/ijd,de->ije/dot_general | solution.py:220
  126.8 0.3 fusion.112
  127.5 0.9 fusion.114
  (122 shorter events, 4.1 us)
Async XLA Ops:
  7.2 32.0 %copy-start = (bf16[256,4096]{1,0:T(8,128)(2,1)S(1)}, bf16[256,4096]{1,0:T(8,128)(2,1)}, u32[]{:S(2)}) copy-start(bf16[256,4096]{1,0:T(8,128)(2,1)} %param.34) | copy-start | bytes 6291460
  7.2 80.0 %all-reduce.4.cloned.1.call-start = ((), (), s32[]{:S(2)}) async-start(), calls=%async_computation | async-start | bytes 1179648 | tf_op jit(solution)/shard_map/psum | solution.py:185
  30.7 2.7 %copy-start.5 = (bf16[192,256]{1,0:T(8,128)(2,1)}, bf16[192,256]{1,0:T(8,128)(2,1)S(1)}, u32[]{:S(2)}) copy-start(bf16[192,256]{1,0:T(8,128)(2,1)S(1)} %all_gather.6) | copy-start | bytes 294916
  32.2 2.3 %copy-start.4 = (f32[3,3,48]{1,0,2:T(4,128)}, f32[3,3,48]{1,0,2:T(4,128)S(1)}, u32[]{:S(2)}) copy-start(f32[3,3,48]{1,0,2:T(4,128)S(1)} %copy.125) | copy-start | bytes 5188
  32.2 4.7 %copy-start.1 = (bf16[48,48,128]{2,1,0:T(8,128)(2,1)S(1)}, bf16[48,48,128]{2,1,0:T(8,128)(2,1)}, u32[]{:S(2)}) copy-start(bf16[48,48,128]{2,1,0:T(8,128)(2,1)} %param.27) | copy-start | bytes 1769476
  36.9 4.2 %copy-start.13 = (s32[48]{0:T(128)S(1)}, s32[48]{0:T(128)}, u32[]{:S(2)}) copy-start(s32[48]{0:T(128)} %get-tuple-element.122) | copy-start | bytes 580
  36.9 4.2 %copy-start.14 = (s32[48]{0:T(128)S(1)}, s32[48]{0:T(128)}, u32[]{:S(2)}) copy-start(s32[48]{0:T(128)} %get-tuple-element.123) | copy-start | bytes 580
  36.9 4.2 %copy-start.9 = (f32[8,48]{1,0:T(8,128)S(1)}, f32[8,48]{1,0:T(8,128)}, u32[]{:S(2)}) copy-start(f32[8,48]{1,0:T(8,128)} %fusion.42) | copy-start | bytes 4612
  38.3 4.0 %copy-start.11 = (f32[48]{0:T(128)S(1)}, f32[48]{0:T(128)}, u32[]{:S(2)}) copy-start(f32[48]{0:T(128)} %get-tuple-element.95) | copy-start | bytes 580
  38.3 4.0 %copy-start.15 = (f32[8]{0:T(128)S(1)}, f32[8]{0:T(128)}, u32[]{:S(2)}) copy-start(f32[8]{0:T(128)} %param.38) | copy-start | bytes 100
  39.1 3.2 %copy-start.3 = (f32[8,48,48]{1,2,0:T(8,128)S(1)}, f32[8,48,48]{1,2,0:T(8,128)}, u32[]{:S(2)}) copy-start(f32[8,48,48]{1,2,0:T(8,128)} %copy.83) | copy-start | bytes 221188
  51.4 22.6 %copy-start.12 = (s32[48]{0:T(128)S(1)}, s32[48]{0:T(128)}, u32[]{:S(2)}) copy-start(s32[48]{0:T(128)} %get-tuple-element.94) | copy-start | bytes 580
  88.3 4.2 %copy-start.10 = (f32[48]{0:T(128)S(1)}, f32[48]{0:T(128)}, u32[]{:S(2)}) copy-start(f32[48]{0:T(128)} %get-tuple-element.93) | copy-start | bytes 580
  89.3 20.1 %copy-start.2 = (bf16[384,128]{1,0:T(8,128)(2,1)S(1)}, bf16[384,128]{1,0:T(8,128)(2,1)}, u32[]{:S(2)}) copy-start(bf16[384,128]{1,0:T(8,128)(2,1)} %param.45) | copy-start | bytes 294916
  89.5 2.4 %copy-start.6 = (bf16[256,256]{1,0:T(8,128)(2,1)S(1)}, bf16[256,256]{1,0:T(8,128)(2,1)}, u32[]{:S(2)}) copy-start(bf16[256,256]{1,0:T(8,128)(2,1)} %param.41) | copy-start | bytes 393220
  89.5 2.4 %copy-start.7 = (bf16[256,256]{1,0:T(8,128)(2,1)S(1)}, bf16[256,256]{1,0:T(8,128)(2,1)}, u32[]{:S(2)}) copy-start(bf16[256,256]{1,0:T(8,128)(2,1)} %param.40) | copy-start | bytes 393220
  92.5 16.9 %copy-start.8 = (bf16[48,256]{1,0:T(8,128)(2,1)}, bf16[48,256]{1,0:T(8,128)(2,1)S(1)}, u32[]{:S(2)}) copy-start(bf16[48,256]{1,0:T(8,128)(2,1)S(1)} %multiply_convert_fusion.1) | copy-start | bytes 73732
Sparse Core Ops, SparseCore 0:
  51.6 35.5 all-reduce.3
where the time goes:
time: 136 us; the launch traced here: 135 us
  blocking collectives  49.1 us (36%)
  matrix products  33.2 us (24%)
  other arithmetic  15.9 us (12%)
  between operations  15.3 us (11%)
  local copies, waits for them, and re-layouts  11.4 us (8%)
  waiting for transfers between devices  10 us (7%)
    psum x1, blocking collectives, body(): summed = lax.psum((denominator, values_out, points_out, pair_sums), 'col')  15.2 us
    all_gather x1, blocking collectives, body(): all_nodes = lax.all_gather(embedded, 'row', axis=0, tiled=True)  15 us
    all_gather x1, blocking collectives, body(): side_all = lax.all_gather(edge_side, 'row', axis=0, tiled=True)  13.2 us
    psum x1, waiting for transfers between devices, body(): summed = lax.psum((denominator, values_out, points_out, pair_sums), 'col')  9.98 us
    dot_general x6, matrix products, edge_block(): jnp.einsum('ijd,de->ije', hidden_one, w_trunk_mid, preferred_element_type...  9.25 us
    pmax x1, blocking collectives, body(): row_peak = lax.pmax(jnp.max(scores, -1), 'col')  5.67 us
    dynamic_update_slice x6, other arithmetic, body(): lax.map(edge_block, (pair_embed.reshape(block_count, block_rows, key_coun...  5.22 us
    dot_general x1, matrix products, node_finish(): framed = jnp.einsum('abi,iahv->ibhv', rotation, relative, precision=highest)  4.51 us
  transfers between devices with their start and end apart: 1, of which 1 were waited for; matrix products, arithmetic and copies ran while one was open for 8% of the time, Pallas kernels for 0%

commit v1 on v0

--- a/solution.py
+++ b/solution.py
@@ -15,6 +15,17 @@
 norm_epsilon = 1e-05
 masked_score = 100000.0
 highest = lax.Precision.HIGHEST
+
+
+def gather_around(shard, axis, dim):
+    ways = lax.axis_size(axis)
+    pieces = [shard]
+    for far in range(1, ways):
+        pieces.append(
+            lax.ppermute(pieces[far - 1], axis, [(d, (d - 1) % ways) for d in range(ways)])
+        )
+    line = jnp.concatenate(pieces, axis=dim)
+    return jnp.roll(line, lax.axis_index(axis) * shard.shape[dim], axis=dim)
 
 
 def layer_norm(values):
@@ -141,7 +152,7 @@
             row_count, 3, HEADS * QP
         ),
     ).reshape(row_count, 3, HEADS, QP)
-    all_nodes = lax.all_gather(embedded, "row", axis=0, tiled=True)
+    all_nodes = gather_around(embedded, "row", 0)
     key_nodes = lax.dynamic_slice_in_dim(all_nodes, key_start, key_count, 0)
     rot_keys = lax.dynamic_slice_in_dim(rotation, key_start, key_count, 2)
     shift_keys = lax.dynamic_slice_in_dim(translation, key_start, key_count, 1)

time: 136 us -> 146 us (1.074)
  waiting for transfers between devices: 10 us -> 32.1 us
  blocking collectives: 49.1 us -> 32.7 us
  starting transfers between devices: 0.04 us -> 7.74 us
  other arithmetic: 15.9 us -> 12.2 us
    psum x1, waiting for transfers between devices: 9.98 us -> 27.1 us  [body(): summed = lax.psum((denominator, values_out, points_out, pair_sums), 'col')]
    all_gather x1 -> x0, blocking collectives: 15 us -> none  [body(): all_nodes = lax.all_gather(embedded, 'row', axis=0, tiled=True)]
    ppermute x0 -> x3, starting transfers between devices: none -> 7.7 us  [gather_around(): lax.ppermute(pieces[far - 1], axis, [(d, (d - 1) % ways) for d in range(w...]
    ppermute x0 -> x3, waiting for transfers between devices: none -> 4.99 us  [gather_around(): lax.ppermute(pieces[far - 1], axis, [(d, (d - 1) % ways) for d in range(w...]
  transfers between devices with their start and end apart: 1 -> 4, of which waited for: 1 -> 3; matrix products, arithmetic and copies ran while one was open for 8% -> 11% of each run, Pallas kernels for 0% -> 0%
where the time goes in v1:
time: 146 us; the launch traced here: 145 us
  blocking collectives  32.7 us (22%)
  matrix products  32.6 us (22%)
  waiting for transfers between devices  32.1 us (22%)
  between operations  15.3 us (10%)
  other arithmetic  12.2 us (8%)
  local copies, waits for them, and re-layouts  12 us (8%)
  starting transfers between devices  7.74 us (5%)
    psum x1, waiting for transfers between devices, body(): summed = lax.psum((denominator, values_out, points_out, pair_sums), 'col')  27.1 us
    psum x1, blocking collectives, body(): summed = lax.psum((denominator, values_out, points_out, pair_sums), 'col')  13.8 us
    all_gather x1, blocking collectives, body(): side_all = lax.all_gather(edge_side, 'row', axis=0, tiled=True)  13.2 us
    dot_general x6, matrix products, edge_block(): jnp.einsum('ijd,de->ije', hidden_one, w_trunk_mid, preferred_element_type...  9.25 us
    ppermute x3, starting transfers between devices, gather_around(): lax.ppermute(pieces[far - 1], axis, [(d, (d - 1) % ways) for d in range(w...  7.7 us
    pmax x1, blocking collectives, body(): row_peak = lax.pmax(jnp.max(scores, -1), 'col')  5.67 us
    dynamic_update_slice x6, other arithmetic, body(): lax.map(edge_block, (pair_embed.reshape(block_count, block_rows, key_coun...  5.22 us
    ppermute x3, waiting for transfers between devices, gather_around(): lax.ppermute(pieces[far - 1], axis, [(d, (d - 1) % ways) for d in range(w...  4.99 us
  transfers between devices with their start and end apart: 4, of which 3 were waited for; matrix products, arithmetic and copies ran while one was open for 11% of the time, Pallas kernels for 0%

profile of v1, /device:TPU:0, one launch (start us, length us, event | category | flops | bytes accessed | tf_op | source)
XLA Modules:
  0.0 145.0 jit_solution(18346088553470720370)
XLA Ops:
  8.1 1.0 fusion.68
  9.2 0.8 add_convert_fusion
  9.9 5.0 %collective-permute-start = (bf16[48,256]{1,0:T(8,128)(2,1)S(1)}, bf16[48,256]{1,0:T(8,128)(2,1)S(1)}, u32[]{:S(2)}, u32[]{:S(2)}) collective-permute-start(bf16[48,256]{1,0:T(8,128)(2,1)S(1)} %add_convert_fusion), channel_id=1, source_target_pairs={{0,12},{4,0},{8,4},{12,8},{1,13},{5,1},{9,5},{13,9},{2,14},{6,2},{... | collective-permute-start | bytes 73736 | tf_op jit(solution)/shard_map/ppermute | solution.py:25
  15.0 0.7 fusion.59
  15.7 0.8 dynamic-slice_bitcast_fusion.4
  16.5 0.9 constant_dynamic-slice_fusion.2
  17.5 1.0 fusion.69
  18.8 0.4 convolution_add_fusion.2
  19.3 2.2 %convolution_convert_fusion.1 = bf16[48,2048]{1,0:T(8,128)(2,1)} fusion(bf16[48,256]{1,0:T(8,128)(2,1)S(1)} %add_convert_fusion, bf16[256,2048]{1,0:T(8,128)(2,1)} %param.32), kind=kOutput, calls=%fused_computation.30 | convolution fusion | flops 50429952 | bytes 1269760 | tf_op jit(solution)/shard_map/dot_general | solution.py:144
  21.7 0.7 fusion.54
  22.8 0.8 copy.83
  23.6 0.4 collective-permute-start.1
  24.0 3.4 %collective-permute-done.1 = bf16[48,256]{1,0:T(8,128)(2,1)S(1)} collective-permute-done((bf16[48,256]{1,0:T(8,128)(2,1)S(1)}, bf16[48,256]{1,0:T(8,128)(2,1)S(1)}, u32[]{:S(2)}, u32[]{:S(2)}) %collective-permute-start.1) | collective-permute-done | bytes 24608 | tf_op jit(solution)/shard_map/ppermute | solution.py:25
  27.4 2.2 %collective-permute-start.2 = (bf16[48,256]{1,0:T(8,128)(2,1)S(1)}, bf16[48,256]{1,0:T(8,128)(2,1)S(1)}, u32[]{:S(2)}, u32[]{:S(2)}) collective-permute-start(bf16[48,256]{1,0:T(8,128)(2,1)S(1)} %collective-permute-done.1), channel_id=1, source_target_pairs={{0,12},{4,0},{8,4},{12,8},{1,13},{5,1},{9,5},{13,9},{2,14},{6,2},{... | collective-permute-start | bytes 73736 | tf_op jit(solution)/shard_map/ppermute | solution.py:25
  29.6 1.6 %collective-permute-done.2 = bf16[48,256]{1,0:T(8,128)(2,1)S(1)} collective-permute-done((bf16[48,256]{1,0:T(8,128)(2,1)S(1)}, bf16[48,256]{1,0:T(8,128)(2,1)S(1)}, u32[]{:S(2)}, u32[]{:S(2)}) %collective-permute-start.2) | collective-permute-done | bytes 24608 | tf_op jit(solution)/shard_map/ppermute | solution.py:25
  31.3 0.7 copy-done.9
  31.9 1.1 fusion.50
  33.2 0.5 convolution_add_fusion.1
  34.0 1.3 convolution_convert_fusion
  35.3 0.7 fusion.63
  36.0 0.5 fusion.27
  36.8 5.7 %pmax.7 = f32[8,48]{1,0:T(8,128)S(1)} all-reduce(f32[8,48]{1,0:T(8,128)S(1)} %get-tuple-element.115), channel_id=1, replica_groups=mesh['groups'=2,'row'=4,'col'=4] {'col'}, use_global_device_ids=true, to_apply=%region_1.2 | all-reduce | flops 384 | bytes 3072 | tf_op jit(solution)/shard_map/pmax | solution.py:183
  42.5 0.3 convolution_bitcast_fusion.1
  43.0 1.2 convolution_bitcast_fusion
  44.2 0.8 copy.131
  44.9 0.3 fusion.70
  45.2 0.7 copy.155
  45.9 13.8 %all-reduce = (f32[48,8]{0,1:T(8,128)S(1)}, f32[48,3,8,12]{0,3,1,2:T(8,128)S(1)}) all-reduce(f32[48,8]{0,1:T(8,128)S(1)} %bitcast.172, f32[48,3,8,12]{0,3,1,2:T(8,128)S(1)} %convolution_bitcast_fusion.1), channel_id=1, replica_groups=mesh['groups'=2,'row'=4,'col'=4] {'col'}, use_global_device_ids=true, to_apply=%region_4.5 | all-reduce | flops 14208 | bytes 113664 | tf_op jit(solution)/shard_map/psum | solution.py:196
  59.8 0.7 divide_subtract_fusion
  60.4 1.8 %copy.97 = f32[48,3,8,12]{3,1,2,0:T(4,128)S(1)} copy(f32[48,3,8,12]{0,3,1,2:T(8,128)} %divide_subtract_fusion) | data formatting | bytes 110592 | tf_op jit(solution)/shard_map/sub | solution.py:75
  62.3 4.5 %multiply_reduce_fusion.1 = (f32[48,8,12]{2,1,0:T(8,128)}, bf16[48,3,8,12]{3,1,2,0:T(4,128)(2,1)}) fusion(f32[48,3,8,12]{3,1,2,0:T(4,128)S(1)} %copy.97, f32[3,3,48]{1,0,2:T(4,128)} %copy-done.5), kind=kOutput, calls=%fused_computation.51 | convolution fusion | flops 534528 | bytes 103104 | tf_op jit(solution)/shard_map/abi,iahv->ibhv/dot_general | solution.py:76
  67.1 1.1 copy.99
  68.3 1.5 %copy.98 = bf16[48,3,8,12]{0,3,2,1:T(8,128)(2,1)S(1)} copy(bf16[48,3,8,12]{3,1,2,0:T(4,128)(2,1)} %get-tuple-element.102) | data formatting | bytes 55296 | tf_op jit(solution)/shard_map/convert.5
  69.9 27.1 %all-reduce.4.cloned.1.call-done = (f32[48,2048]{1,0:T(8,128)}, f32[48,1024]{1,0:T(8,128)}) async-done(((f32[48,2048]{1,0:T(8,128)}, f32[48,1024]{1,0:T(8,128)}), (f32[48,2048]{1,0:T(8,128)}, f32[48,1024]{1,0:T(8,128)})) %all-reduce.4.cloned.1.call-update) | async-done | bytes 589840 | tf_op jit(solution)/shard_map/psum | solution.py:196
  97.1 1.0 fusion.29
  98.1 1.1 divide_convert_fusion
  99.3 2.0 %fusion.66 = (f32[48]{0:T(128)S(1)}, f32[48,256]{1,0:T(8,128)S(1)}) fusion(bf16[48,3456]{1,0:T(8,128)(2,1)S(1)} %concatenate.21, bf16[3456,256]{1,0:T(8,128)(2,1)} %param.39, bf16[48,256]{1,0:T(8,128)(2,1)S(1)} %add_convert_fusion), kind=kOutput, calls=%fused_computation.128 | convolution fusion | flops 84971472 | bytes 2175168 | tf_op jit(solution)/shard_map/dot_general | solution.py:88
  101.6 0.4 fusion.67
  102.3 1.0 convolution_convert_fusion.2
  103.3 13.2 %all_gather.3 = bf16[192,128]{1,0:T(8,128)(2,1)S(1)} all-gather(bf16[48,128]{1,0:T(8,128)(2,1)S(1)} %convolution_convert_fusion.2), channel_id=1, replica_groups=mesh['groups'=2,'row'=4,'col'=4] {'row'}, dimensions={0}, use_global_device_ids=true | all-gather | bytes 61440 | tf_op jit(solution)/shard_map/all_gather | solution.py:211
  116.5 1.0 convolution_bitcast_fusion.3
  117.5 1.7 %fusion.44 = f32[48,384]{1,0:T(8,128)} fusion(bf16[48,128]{1,0:T(8,128)(2,1)S(1)} %get-tuple-element.215, bf16[384,384]{1,0:T(8,128)(2,1)} %param.43), kind=kOutput, calls=%fused_computation.74 | convolution fusion | flops 4718592 | bytes 184320 | tf_op jit(solution)/shard_map/dot_general | solution.py:215
  119.2 18.9 %while.10 = (s32[]{:T(128)}, bf16[6,8,48,128]{3,2,1,0:T(8,128)(2,1)}, bf16[6,8,48,128]{3,2,1,0:T(8,128)(2,1)S(1)}, bf16[384,384]{1,0:T(8,128)(2,1)}, f32[6,8,384...) while((s32[]{:T(128)}, ...), condition=%wide.region_15.16_spmd, body=%wide.region_12.15_spmd.sunk | while | flops 191054592 | bytes 2702265 | solution.py:246
  119.3 1.5 %fusion.111 = bf16[8,48,384]{2,1,0:T(8,128)(2,1)S(1)} fusion(bf16[8,48,128]{2,1,0:T(8,128)(2,1)S(1)} %dynamic-slice_bitcast_fusion.9, bf16[8,48,128]{2,1,0:T(8,128)(2,1)S(1)} %broadcast_in_dim.14, bf16[8,48,128]{2,1,0:T(8,128)(2,1)S(1)} %broadcast_in_dim.15, bf16[384,384]{1,0:T(8,128)(2,1)} %get-tuple-element.239, f32[48,384]{1,0:T(8,128)} %get-tuple-element.238, ...), kind=kOutput, calls=%fused_computation.6.clone.1 | convolution fusion | flops 152911872 | bytes 1167360 | tf_op jit(solution)/shard_map/while/body/eval_jaxpr/ijd,de->ije/dot_general | solution.py:231
  120.9 0.3 fusion.112
  121.2 0.2 multiply_reduce_fusion.6
  121.5 0.9 fusion.114
  122.5 1.5 %fusion.111 = bf16[8,48,384]{2,1,0:T(8,128)(2,1)S(1)} fusion(bf16[8,48,128]{2,1,0:T(8,128)(2,1)S(1)} %dynamic-slice_bitcast_fusion.9, bf16[8,48,128]{2,1,0:T(8,128)(2,1)S(1)} %broadcast_in_dim.14, bf16[8,48,128]{2,1,0:T(8,128)(2,1)S(1)} %broadcast_in_dim.15, bf16[384,384]{1,0:T(8,128)(2,1)} %get-tuple-element.239, f32[48,384]{1,0:T(8,128)} %get-tuple-element.238, ...), kind=kOutput, calls=%fused_computation.6.clone.1 | convolution fusion | flops 152911872 | bytes 1167360 | tf_op jit(solution)/shard_map/while/body/eval_jaxpr/ijd,de->ije/dot_general | solution.py:231
  124.0 0.3 fusion.112
  124.4 0.2 multiply_reduce_fusion.6
  124.7 0.9 fusion.114
  125.6 1.5 %fusion.111 = bf16[8,48,384]{2,1,0:T(8,128)(2,1)S(1)} fusion(bf16[8,48,128]{2,1,0:T(8,128)(2,1)S(1)} %dynamic-slice_bitcast_fusion.9, bf16[8,48,128]{2,1,0:T(8,128)(2,1)S(1)} %broadcast_in_dim.14, bf16[8,48,128]{2,1,0:T(8,128)(2,1)S(1)} %broadcast_in_dim.15, bf16[384,384]{1,0:T(8,128)(2,1)} %get-tuple-element.239, f32[48,384]{1,0:T(8,128)} %get-tuple-element.238, ...), kind=kOutput, calls=%fused_computation.6.clone.1 | convolution fusion | flops 152911872 | bytes 1167360 | tf_op jit(solution)/shard_map/while/body/eval_jaxpr/ijd,de->ije/dot_general | solution.py:231
  127.2 0.3 fusion.112
  127.5 0.2 multiply_reduce_fusion.6
  127.8 0.9 fusion.114
  128.8 1.5 %fusion.111 = bf16[8,48,384]{2,1,0:T(8,128)(2,1)S(1)} fusion(bf16[8,48,128]{2,1,0:T(8,128)(2,1)S(1)} %dynamic-slice_bitcast_fusion.9, bf16[8,48,128]{2,1,0:T(8,128)(2,1)S(1)} %broadcast_in_dim.14, bf16[8,48,128]{2,1,0:T(8,128)(2,1)S(1)} %broadcast_in_dim.15, bf16[384,384]{1,0:T(8,128)(2,1)} %get-tuple-element.239, f32[48,384]{1,0:T(8,128)} %get-tuple-element.238, ...), kind=kOutput, calls=%fused_computation.6.clone.1 | convolution fusion | flops 152911872 | bytes 1167360 | tf_op jit(solution)/shard_map/while/body/eval_jaxpr/ijd,de->ije/dot_general | solution.py:231
  130.3 0.3 fusion.112
  131.0 0.9 fusion.114
  131.9 1.5 %fusion.111 = bf16[8,48,384]{2,1,0:T(8,128)(2,1)S(1)} fusion(bf16[8,48,128]{2,1,0:T(8,128)(2,1)S(1)} %dynamic-slice_bitcast_fusion.9, bf16[8,48,128]{2,1,0:T(8,128)(2,1)S(1)} %broadcast_in_dim.14, bf16[8,48,128]{2,1,0:T(8,128)(2,1)S(1)} %broadcast_in_dim.15, bf16[384,384]{1,0:T(8,128)(2,1)} %get-tuple-element.239, f32[48,384]{1,0:T(8,128)} %get-tuple-element.238, ...), kind=kOutput, calls=%fused_computation.6.clone.1 | convolution fusion | flops 152911872 | bytes 1167360 | tf_op jit(solution)/shard_map/while/body/eval_jaxpr/ijd,de->ije/dot_general | solution.py:231
  133.5 0.3 fusion.112
  134.1 0.9 fusion.114
  135.1 1.5 %fusion.111 = bf16[8,48,384]{2,1,0:T(8,128)(2,1)S(1)} fusion(bf16[8,48,128]{2,1,0:T(8,128)(2,1)S(1)} %dynamic-slice_bitcast_fusion.9, bf16[8,48,128]{2,1,0:T(8,128)(2,1)S(1)} %broadcast_in_dim.14, bf16[8,48,128]{2,1,0:T(8,128)(2,1)S(1)} %broadcast_in_dim.15, bf16[384,384]{1,0:T(8,128)(2,1)} %get-tuple-element.239, f32[48,384]{1,0:T(8,128)} %get-tuple-element.238, ...), kind=kOutput, calls=%fused_computation.6.clone.1 | convolution fusion | flops 152911872 | bytes 1167360 | tf_op jit(solution)/shard_map/while/body/eval_jaxpr/ijd,de->ije/dot_general | solution.py:231
  136.6 0.3 fusion.112
  137.3 0.9 fusion.114
  (131 shorter events, 4.8 us)
Async XLA Ops:
  7.2 26.8 %copy-start = (bf16[256,4096]{1,0:T(8,128)(2,1)S(1)}, bf16[256,4096]{1,0:T(8,128)(2,1)}, u32[]{:S(2)}) copy-start(bf16[256,4096]{1,0:T(8,128)(2,1)} %param.34) | copy-start | bytes 6291460
  7.2 14.4 %copy-start.11 = (s32[192]{0:T(256)S(1)}, s32[192]{0:T(256)}, u32[]{:S(2)}) copy-start(s32[192]{0:T(256)} %param.29) | copy-start | bytes 2308
  7.2 14.4 %copy-start.12 = (s32[192]{0:T(256)S(1)}, s32[192]{0:T(256)}, u32[]{:S(2)}) copy-start(s32[192]{0:T(256)} %param.28) | copy-start | bytes 2308
  7.2 14.5 %copy-start.1 = (bf16[48,48,128]{2,1,0:T(8,128)(2,1)S(1)}, bf16[48,48,128]{2,1,0:T(8,128)(2,1)}, u32[]{:S(2)}) copy-start(bf16[48,48,128]{2,1,0:T(8,128)(2,1)} %param.27) | copy-start | bytes 1769476
  7.2 14.5 %copy-start.10 = (bf16[128,8]{0,1:T(8,128)(2,1)S(1)}, bf16[128,8]{0,1:T(8,128)(2,1)}, u32[]{:S(2)}) copy-start(bf16[128,8]{0,1:T(8,128)(2,1)} %param.36) | copy-start | bytes 6148
  7.2 89.8 %all-reduce.4.cloned.1.call-start = ((), (), s32[]{:S(2)}) async-start(), calls=%async_computation | async-start | bytes 1179648 | tf_op jit(solution)/shard_map/psum | solution.py:196
  9.9 13.6 %collective-permute-start = (bf16[48,256]{1,0:T(8,128)(2,1)S(1)}, bf16[48,256]{1,0:T(8,128)(2,1)S(1)}, u32[]{:S(2)}, u32[]{:S(2)}) collective-permute-start(bf16[48,256]{1,0:T(8,128)(2,1)S(1)} %add_convert_fusion), channel_id=1, source_target_pairs={{0,12},{4,0},{8,4},{12,8},{1,13},{5,1},{9,5},{13,9},{2,14},{6,2},{... | collective-permute-start | bytes 73736 | tf_op jit(solution)/shard_map/ppermute | solution.py:25
  18.7 2.9 %copy-start.5 = (f32[3,3,48]{1,0,2:T(4,128)}, f32[3,3,48]{1,0,2:T(4,128)S(1)}, u32[]{:S(2)}) copy-start(f32[3,3,48]{1,0,2:T(4,128)S(1)} %copy.125) | copy-start | bytes 5188
  23.6 3.8 %collective-permute-start.1 = (bf16[48,256]{1,0:T(8,128)(2,1)S(1)}, bf16[48,256]{1,0:T(8,128)(2,1)S(1)}, u32[]{:S(2)}, u32[]{:S(2)}) collective-permute-start(bf16[48,256]{1,0:T(8,128)(2,1)S(1)} %collective-permute-done), channel_id=1, source_target_pairs={{0,12},{4,0},{8,4},{12,8},{1,13},{5,1},{9,5},{13,9},{2,14},{6,2},{... | collective-permute-start | bytes 73736 | tf_op jit(solution)/shard_map/ppermute | solution.py:25
  27.4 3.8 %collective-permute-start.2 = (bf16[48,256]{1,0:T(8,128)(2,1)S(1)}, bf16[48,256]{1,0:T(8,128)(2,1)S(1)}, u32[]{:S(2)}, u32[]{:S(2)}) collective-permute-start(bf16[48,256]{1,0:T(8,128)(2,1)S(1)} %collective-permute-done.1), channel_id=1, source_target_pairs={{0,12},{4,0},{8,4},{12,8},{1,13},{5,1},{9,5},{13,9},{2,14},{6,2},{... | collective-permute-start | bytes 73736 | tf_op jit(solution)/shard_map/ppermute | solution.py:25
  31.3 0.7 copy-start.9
  33.9 2.7 %copy-start.13 = (f32[8]{0:T(128)S(1)}, f32[8]{0:T(128)}, u32[]{:S(2)}) copy-start(f32[8]{0:T(128)} %param.38) | copy-start | bytes 100
  33.9 2.6 %copy-start.3 = (bf16[48,2048]{1,0:T(8,128)(2,1)S(1)}, bf16[48,2048]{1,0:T(8,128)(2,1)}, u32[]{:S(2)}) copy-start(bf16[48,2048]{1,0:T(8,128)(2,1)} %convolution_convert_fusion.1) | copy-start | bytes 589828
  33.9 2.6 %copy-start.4 = (f32[8,48,48]{1,2,0:T(8,128)S(1)}, f32[8,48,48]{1,2,0:T(8,128)}, u32[]{:S(2)}) copy-start(f32[8,48,48]{1,2,0:T(8,128)} %copy.83) | copy-start | bytes 221188
  99.1 20.1 %copy-start.2 = (bf16[384,128]{1,0:T(8,128)(2,1)S(1)}, bf16[384,128]{1,0:T(8,128)(2,1)}, u32[]{:S(2)}) copy-start(bf16[384,128]{1,0:T(8,128)(2,1)} %param.45) | copy-start | bytes 294916
  99.3 2.4 %copy-start.6 = (bf16[256,256]{1,0:T(8,128)(2,1)S(1)}, bf16[256,256]{1,0:T(8,128)(2,1)}, u32[]{:S(2)}) copy-start(bf16[256,256]{1,0:T(8,128)(2,1)} %param.41) | copy-start | bytes 393220
  99.3 2.4 %copy-start.7 = (bf16[256,256]{1,0:T(8,128)(2,1)S(1)}, bf16[256,256]{1,0:T(8,128)(2,1)}, u32[]{:S(2)}) copy-start(bf16[256,256]{1,0:T(8,128)(2,1)} %param.40) | copy-start | bytes 393220
  102.3 16.9 %copy-start.8 = (bf16[48,256]{1,0:T(8,128)(2,1)}, bf16[48,256]{1,0:T(8,128)(2,1)S(1)}, u32[]{:S(2)}) copy-start(bf16[48,256]{1,0:T(8,128)(2,1)S(1)} %multiply_convert_fusion.1) | copy-start | bytes 73732
Sparse Core Ops, SparseCore 0:
  62.4 34.5 all-reduce.3
